TPU v7x, 32 devices: a whole 2x2x4 slice. The times are simulated.
32 devices in a mesh: dp: 2 (over y), expert: 16 (over z, x, core).
Axes of the slice: x: 2, y: 2, z: 4, core: 2. Of those that a mesh axis runs over, the one named last changes fastest.
Arguments:
- tokens: bfloat16 [1024, 2048], P(('dp', 'expert')), may hold values from -6 to 6
- routes: int32 [1024, 8], P(('dp', 'expert')), may hold values from 0 to 15, all different within a row; in each aligned block of 32 rows (0 to 31, 32 to 63, ...) at most 32 rows name the same one
- cotangent: bfloat16 [1024, 2048], P(('dp', 'expert')), may hold values from -6 to 6
- router_weight: bfloat16 [2048, 16], replicated, may hold values from -0.375 to 0.375
- gate_weight: bfloat16 [16, 2048, 768], P('expert'), may hold values from -0.125 to 0.125
- up_weight: bfloat16 [16, 2048, 768], P('expert'), may hold values from -0.125 to 0.125
- down_weight: bfloat16 [16, 768, 2048], P('expert'), may hold values from -0.21875 to 0.21875
Outputs:
- layer_out: bfloat16 [1024, 2048], P(('dp', 'expert'))
- token_grad: bfloat16 [1024, 2048], P(('dp', 'expert'))
- gate_grad: bfloat16 [16, 2048, 768], P('expert', 'dp')
- up_grad: bfloat16 [16, 2048, 768], P('expert', 'dp')
- down_grad: bfloat16 [16, 768, 2048], P('expert', None, 'dp')
- router_grad: float32 [2048, 16], replicated
Inputs may be any that keep to these rules, and one draw needn't show every extreme that they name: `routes`: each row names 8 different experts. Among the 32 rows of one device no expert is named by more than 32 rows, and in some device's rows an expert is named by exactly 32 rows.
All inputs are finite; a program needn't handle non-finite values.
Results may differ from a plain program's by a relative error of at most 0.0061.
Values may be sent and summed in bfloat16 or wider, within the bound.
A program may use at most 128 MiB of HBM per device.

v0:
```python
import jax
import jax.numpy as jnp
from jax import lax
from jax.sharding import PartitionSpec as P


def silu_parts(gate_act):
    sigmoid_value = jax.nn.sigmoid(gate_act)
    act_value = gate_act * sigmoid_value
    act_slope = sigmoid_value * (1.0 + gate_act * (1.0 - sigmoid_value))
    return (act_value, act_slope)


def expert_forward(arrived, gate_weight, up_weight, down_weight):
    gate_act = jnp.einsum(
        "sjcd,jdf->sjcf", arrived, gate_weight, preferred_element_type=jnp.float32
    )
    up_act = jnp.einsum("sjcd,jdf->sjcf", arrived, up_weight, preferred_element_type=jnp.float32)
    act_value, act_slope = silu_parts(gate_act)
    hidden = (act_value * up_act).astype(jnp.bfloat16)
    expert_out = jnp.einsum(
        "sjcf,jfd->sjcd", hidden, down_weight, preferred_element_type=jnp.float32
    ).astype(jnp.bfloat16)
    return (expert_out, (up_act, act_value, act_slope, hidden))


def expert_backward(arrived_grads, stored, gate_weight, up_weight, down_weight):
    up_act, act_value, act_slope, hidden = stored
    hidden_grad = jnp.einsum(
        "sjcd,jfd->sjcf", arrived_grads, down_weight, preferred_element_type=jnp.float32
    )
    gate_part = (hidden_grad * up_act * act_slope).astype(jnp.bfloat16)
    up_part = (hidden_grad * act_value).astype(jnp.bfloat16)
    input_grad = (
        jnp.einsum("sjcf,jdf->sjcd", gate_part, gate_weight, preferred_element_type=jnp.float32)
        + jnp.einsum("sjcf,jdf->sjcd", up_part, up_weight, preferred_element_type=jnp.float32)
    ).astype(jnp.bfloat16)
    return (input_grad, gate_part, up_part)


def local(tokens, routes, cotangent, router_weight, gate_weight, up_weight, down_weight):
    tok_rows, top_count = routes.shape
    model_width = tokens.shape[1]
    expert_count = router_weight.shape[1]
    local_count = gate_weight.shape[0]
    group_size = lax.axis_size("expert")
    capacity = min(tok_rows, 2 * tok_rows * top_count // expert_count)
    slot_total = expert_count * capacity
    buffer_shape = (group_size, local_count, capacity, model_width)
    logits = jnp.dot(tokens, router_weight, preferred_element_type=jnp.float32)
    exp_logits = jnp.exp(logits)
    probability = exp_logits / jnp.sum(exp_logits, axis=1, keepdims=True)
    chosen = (
        routes[:, :, None] == jnp.arange(expert_count, dtype=jnp.int32)[None, None, :]
    ).astype(jnp.int32)
    chosen_float = chosen.astype(jnp.float32)
    selected = jnp.sum(chosen_float * probability[:, None, :], axis=2)
    sel_total = jnp.sum(selected, axis=1, keepdims=True)
    combine = selected / sel_total
    per_token = jnp.sum(chosen, axis=1)
    earlier = jnp.cumsum(per_token, axis=0) - per_token
    slot_ids = jnp.sum(chosen * earlier[:, None, :], axis=2)
    flat_slot = routes * capacity + slot_ids
    match_map = (
        flat_slot[:, :, None] == jnp.arange(slot_total, dtype=jnp.int32)[None, None, :]
    ).astype(jnp.float32)
    presence = jnp.sum(match_map, axis=1)
    weight_map = jnp.sum(match_map * combine[:, :, None], axis=1)
    send_rows = (
        jnp.einsum(
            "tr,td->rd", presence.astype(jnp.bfloat16), tokens, preferred_element_type=jnp.float32
        )
        .astype(jnp.bfloat16)
        .reshape(buffer_shape)
    )
    send_grads = (
        jnp.einsum(
            "tr,td->rd", weight_map, cotangent.astype(jnp.float32), precision=lax.Precision.HIGHEST
        )
        .astype(jnp.bfloat16)
        .reshape(buffer_shape)
    )
    arrived = lax.all_to_all(send_rows, "expert", split_axis=0, concat_axis=0, tiled=True)
    expert_out, stored = expert_forward(arrived, gate_weight, up_weight, down_weight)
    returned = lax.all_to_all(expert_out, "expert", split_axis=0, concat_axis=0, tiled=True)
    arrived_grads = lax.all_to_all(send_grads, "expert", split_axis=0, concat_axis=0, tiled=True)
    input_grad, gate_part, up_part = expert_backward(
        arrived_grads, stored, gate_weight, up_weight, down_weight
    )
    returned_grads = lax.all_to_all(input_grad, "expert", split_axis=0, concat_axis=0, tiled=True)
    hidden = stored[3]
    gate_term = jnp.einsum("sjcd,sjcf->jdf", arrived, gate_part, preferred_element_type=jnp.float32)
    up_term = jnp.einsum("sjcd,sjcf->jdf", arrived, up_part, preferred_element_type=jnp.float32)
    down_term = jnp.einsum(
        "sjcf,sjcd->jfd", hidden, arrived_grads, preferred_element_type=jnp.float32
    )
    gate_sum, up_sum, down_sum = (
        lax.psum_scatter(gate_term, "dp", scatter_dimension=1, tiled=True),
        lax.psum_scatter(up_term, "dp", scatter_dimension=1, tiled=True),
        lax.psum_scatter(down_term, "dp", scatter_dimension=2, tiled=True),
    )
    gate_grad = gate_sum.astype(jnp.bfloat16)
    up_grad = up_sum.astype(jnp.bfloat16)
    down_grad = down_sum.astype(jnp.bfloat16)
    flat_index = flat_slot.reshape(-1)
    out_sel = jnp.take(returned.reshape(slot_total, model_width), flat_index, axis=0).reshape(
        tok_rows, top_count, model_width
    )
    grad_sel = jnp.take(
        returned_grads.reshape(slot_total, model_width), flat_index, axis=0
    ).reshape(tok_rows, top_count, model_width)
    layer_out = jnp.sum(combine[:, :, None] * out_sel.astype(jnp.float32), axis=1).astype(
        jnp.bfloat16
    )
    comb_grad = jnp.einsum("tkd,td->tk", out_sel, cotangent, preferred_element_type=jnp.float32)
    sel_grad = (comb_grad - jnp.sum(combine * comb_grad, axis=1, keepdims=True)) / sel_total
    prob_grad = jnp.sum(chosen_float * sel_grad[:, :, None], axis=1)
    logit_grad = probability * (prob_grad - jnp.sum(probability * prob_grad, axis=1, keepdims=True))
    router_term = jnp.einsum(
        "td,te->de", tokens.astype(jnp.float32), logit_grad, precision=lax.Precision.HIGHEST
    )
    router_grad = lax.psum(router_term, ("dp", "expert"))
    router_back = jnp.einsum(
        "te,de->td", logit_grad, router_weight.astype(jnp.float32), precision=lax.Precision.HIGHEST
    )
    token_grad = (jnp.sum(grad_sel.astype(jnp.float32), axis=1) + router_back).astype(jnp.bfloat16)
    return (layer_out, token_grad, gate_grad, up_grad, down_grad, router_grad)


def solution(mesh):
    return jax.shard_map(
        local,
        mesh=mesh,
        in_specs=(
            P(("dp", "expert"), None),
            P(("dp", "expert"), None),
            P(("dp", "expert"), None),
            P(),
            P("expert", None, None),
            P("expert", None, None),
            P("expert", None, None),
        ),
        out_specs=(
            P(("dp", "expert"), None),
            P(("dp", "expert"), None),
            P("expert", "dp", None),
            P("expert", "dp", None),
            P("expert", None, "dp"),
            P(),
        ),
        check_vma=False,
    )
```

profile of v0, /device:TPU:0, one launch (start us, length us, event | category | flops | bytes accessed | tf_op | source)
XLA Modules:
  0.0 455.1 jit_solution(14684139448227573478)
XLA Ops:
  8.9 1.1 fusion.55
  12.9 4.0 convolution_convert_fusion
  16.9 7.5 %all-to-all-start.2 = ((bf16[16,1,32,2048]{3,2,1,0:T(8,128)(2,1)}), bf16[16,1,32,2048]{3,2,1,0:T(8,128)(2,1)}, u32[]{:S(2)}, u32[]{:S(2)}) async-start(bf16[16,1,32,2048]{3,2,1,0:T(8,128)(2,1)} %bitcast.170), calls=%async_computation.2 | async-start | bytes 4194304 | tf_op jit(solution)/shard_map/all_to_all | solution.py:86
  24.5 2.1 convolution_convert_fusion.1
  26.6 39.1 %all-to-all-done.2 = bf16[16,1,32,2048]{3,2,1,0:T(8,128)(2,1)} async-done(((bf16[16,1,32,2048]{3,2,1,0:T(8,128)(2,1)}), bf16[16,1,32,2048]{3,2,1,0:T(8,128)(2,1)}, u32[]{:S(2)}, u32[]{:S(2)}) %all-to-all-start.2) | async-done | bytes 2097184 | tf_op jit(solution)/shard_map/all_to_all | solution.py:86
  65.7 11.3 %all-to-all-start = ((bf16[16,1,32,2048]{3,2,1,0:T(8,128)(2,1)}), bf16[16,1,32,2048]{3,2,1,0:T(8,128)(2,1)}, u32[]{:S(2)}, u32[]{:S(2)}) async-start(bf16[16,1,32,2048]{3,2,1,0:T(8,128)(2,1)} %bitcast.169), calls=%async_computation | async-start | bytes 4194304 | tf_op jit(solution)/shard_map/all_to_all | solution.py:83
  77.0 5.5 %fusion = f32[16,32,768]{2,1,0:T(8,128)} fusion(bf16[1,768,2048]{2,1,0:T(8,128)(2,1)} %param.15, bf16[16,1,32,2048]{3,2,1,0:T(8,128)(2,1)} %all-to-all-done.2), kind=kOutput, calls=%fused_computation.6 | convolution fusion | flops 1610612736 | bytes 6815744 | tf_op jit(solution)/shard_map/sjcd,jfd->sjcf/dot_general | solution.py:29
  82.5 35.6 %all-to-all-done = bf16[16,1,32,2048]{3,2,1,0:T(8,128)(2,1)} async-done(((bf16[16,1,32,2048]{3,2,1,0:T(8,128)(2,1)}), bf16[16,1,32,2048]{3,2,1,0:T(8,128)(2,1)}, u32[]{:S(2)}, u32[]{:S(2)}) %all-to-all-start) | async-done | bytes 2097184 | tf_op jit(solution)/shard_map/all_to_all | solution.py:83
  118.1 4.4 fusion.6
  122.5 5.1 %fusion.41 = (bf16[16,32,768]{2,1,0:T(8,128)(2,1)S(1)}, bf16[16,1,32,768]{3,2,0,1:T(8,128)(2,1)}, bf16[16,32,768]{2,1,0:T(8,128)(2,1)}) fusion(f32[16,32,768]{2,1,0:T(8,128)S(1)} %fusion.6, f32[16,32,768]{2,1,0:T(8,128)S(1)} %copy-done.6, bf16[1,2048,768]{2,1,0:T(8,128)(2,1)S(1)} %copy-done, bf16[16,1,32,2048]{3,2,1,0:T(8,128)(2,1)} %all-to-all-done), kind=kOutput, calls=%fused_computation.53 | convolution fusion | flops 1616510976 | bytes 10747904 | tf_op jit(solution)/shard_map/sjcd,jdf->sjcf/dot_general | solution.py:15
  128.5 6.1 %convolution_bitcast_fusion = f32[1,768,2048]{2,1,0:T(8,128)} fusion(bf16[16,32,768]{2,1,0:T(8,128)(2,1)S(1)} %get-tuple-element.13, bf16[16,1,32,2048]{3,2,1,0:T(8,128)(2,1)} %all-to-all-done.2), kind=kOutput, calls=%fused_computation.3 | convolution fusion | flops 1610612736 | bytes 9175040 | tf_op jit(solution)/shard_map/sjcf,sjcd->jfd/dot_general | solution.py:94
  134.7 6.3 %convolution_bitcast_fusion.2 = f32[1,2048,768]{2,1,0:T(8,128)} fusion(bf16[16,1,32,2048]{3,2,1,0:T(8,128)(2,1)} %all-to-all-done, bf16[16,1,32,768]{3,2,0,1:T(8,128)(2,1)} %get-tuple-element.14), kind=kOutput, calls=%fused_computation.5 | convolution fusion | flops 1610612736 | bytes 9175040 | tf_op jit(solution)/shard_map/sjcd,sjcf->jdf/dot_general | solution.py:92
  141.2 6.3 %convolution_bitcast_fusion.1 = f32[1,2048,768]{2,1,0:T(8,128)} fusion(bf16[16,32,768]{2,1,0:T(8,128)(2,1)} %get-tuple-element.15, bf16[16,1,32,2048]{3,2,1,0:T(8,128)(2,1)} %all-to-all-done), kind=kOutput, calls=%fused_computation.4 | convolution fusion | flops 1610612736 | bytes 9175040 | tf_op jit(solution)/shard_map/sjcd,sjcf->jdf/dot_general | solution.py:93
  147.5 5.6 %fusion.17 = bf16[16,1,32,2048]{3,2,1,0:T(8,128)(2,1)} fusion(bf16[16,32,768]{2,1,0:T(8,128)(2,1)} %copy-done.7, bf16[1,768,2048]{2,1,0:T(8,128)(2,1)} %param.15), kind=kOutput, calls=%fused_computation.21 | convolution fusion | flops 1611661312 | bytes 6029312 | tf_op jit(solution)/shard_map/sjcf,jfd->sjcd/dot_general | solution.py:21
  153.1 11.6 %all-to-all-start.1 = ((bf16[16,1,32,2048]{3,2,1,0:T(8,128)(2,1)}), bf16[16,1,32,2048]{3,2,1,0:T(8,128)(2,1)}, u32[]{:S(2)}, u32[]{:S(2)}) async-start(bf16[16,1,32,2048]{3,2,1,0:T(8,128)(2,1)} %fusion.17), calls=%async_computation.1 | async-start | bytes 4194304 | tf_op jit(solution)/shard_map/all_to_all | solution.py:85
  164.8 4.0 fusion.4
  168.8 3.1 fusion.20
  171.9 34.0 %all-to-all-done.1 = bf16[16,1,32,2048]{3,2,1,0:T(8,128)(2,1)} async-done(((bf16[16,1,32,2048]{3,2,1,0:T(8,128)(2,1)}), bf16[16,1,32,2048]{3,2,1,0:T(8,128)(2,1)}, u32[]{:S(2)}, u32[]{:S(2)}) %all-to-all-start.1) | async-done | bytes 2097184 | tf_op jit(solution)/shard_map/all_to_all | solution.py:85
  205.9 11.3 %all-to-all-start.3 = ((bf16[16,1,32,2048]{3,2,1,0:T(8,128)(2,1)}), bf16[16,1,32,2048]{3,2,1,0:T(8,128)(2,1)}, u32[]{:S(2)}, u32[]{:S(2)}) async-start(bf16[16,1,32,2048]{3,2,1,0:T(8,128)(2,1)} %fusion.20), calls=%async_computation.3 | async-start | bytes 4194304 | tf_op jit(solution)/shard_map/all_to_all | solution.py:90
  217.4 5.3 %gather_fusion = bf16[256,2048]{1,0:T(8,128)(2,1)} fusion(bf16[512,2048]{1,0:T(8,128)(2,1)} %bitcast.22, s32[1024]{0:T(1024)S(1)} %pad_clamp_fusion), kind=kCustom, calls=%fused_computation.clone | custom fusion | bytes 2098176 | tf_op jit(solution)/shard_map/jit(_take)/gather | solution.py:106
  222.7 2.1 fusion.39
  224.9 33.4 %all-to-all-done.3 = bf16[16,1,32,2048]{3,2,1,0:T(8,128)(2,1)} async-done(((bf16[16,1,32,2048]{3,2,1,0:T(8,128)(2,1)}), bf16[16,1,32,2048]{3,2,1,0:T(8,128)(2,1)}, u32[]{:S(2)}, u32[]{:S(2)}) %all-to-all-start.3) | async-done | bytes 2097184 | tf_op jit(solution)/shard_map/all_to_all | solution.py:90
  258.3 5.2 %gather_fusion.1 = bf16[256,2048]{1,0:T(8,128)(2,1)} fusion(bf16[512,2048]{1,0:T(8,128)(2,1)} %bitcast.40, s32[1024]{0:T(1024)S(1)} %pad_clamp_fusion), kind=kCustom, calls=%fused_computation.1.clone | custom fusion | bytes 2098176 | tf_op jit(solution)/shard_map/jit(_take)/gather | solution.py:109
  264.5 4.0 convert_reduce_fusion
  268.5 1.0 fusion.23
  269.5 3.3 convert_element_type.102
  272.7 25.2 %reduce-scatter.4.cloned.1.call-done = f32[1,1024,768]{2,1,0:T(8,128)} async-done(((f32[1,2048,768]{2,1,0:T(8,128)}), f32[1,1024,768]{2,1,0:T(8,128)}) %reduce-scatter.4.cloned.1.call-update) | async-done | bytes 3145744 | tf_op jit(solution)/shard_map/reduce_scatter | solution.py:98
  297.9 3.2 convert_element_type.100
  301.1 76.4 %reduce-scatter.6.cloned.1.call-done = f32[1,1024,768]{2,1,0:T(8,128)} async-done(((f32[1,2048,768]{2,1,0:T(8,128)}), f32[1,1024,768]{2,1,0:T(8,128)}) %reduce-scatter.6.cloned.1.call-update) | async-done | bytes 3145744 | tf_op jit(solution)/shard_map/reduce_scatter | solution.py:99
  377.6 3.2 convert_element_type.101
  380.8 65.6 %all-reduce.2.cloned.1.call-done = f32[2048,16]{0,1:T(8,128)} async-done(((f32[2048,16]{0,1:T(8,128)}), f32[2048,16]{0,1:T(8,128)}) %all-reduce.2.cloned.1.call-update) | async-done | bytes 131088 | tf_op jit(solution)/shard_map/psum | solution.py:122
  446.4 1.6 copy.44
  (48 shorter events, 6.2 us)
Async XLA Ops:
  8.0 114.5 %copy-start = (bf16[1,2048,768]{2,1,0:T(8,128)(2,1)S(1)}, bf16[1,2048,768]{2,1,0:T(8,128)(2,1)}, u32[]{:S(2)}) copy-start(bf16[1,2048,768]{2,1,0:T(8,128)(2,1)} %param.13) | copy-start | bytes 9437188
  16.9 7.6 %copy-start.1 = (bf16[32,2048]{1,0:T(8,128)(2,1)S(1)}, bf16[32,2048]{1,0:T(8,128)(2,1)}, u32[]{:S(2)}) copy-start(bf16[32,2048]{1,0:T(8,128)(2,1)} %param.9) | copy-start | bytes 393220
  16.9 48.7 %all-to-all-start.2 = ((bf16[16,1,32,2048]{3,2,1,0:T(8,128)(2,1)}), bf16[16,1,32,2048]{3,2,1,0:T(8,128)(2,1)}, u32[]{:S(2)}, u32[]{:S(2)}) async-start(bf16[16,1,32,2048]{3,2,1,0:T(8,128)(2,1)} %bitcast.170), calls=%async_computation.2 | async-start | bytes 4194304 | tf_op jit(solution)/shard_map/all_to_all | solution.py:86
  65.7 52.4 %all-to-all-start = ((bf16[16,1,32,2048]{3,2,1,0:T(8,128)(2,1)}), bf16[16,1,32,2048]{3,2,1,0:T(8,128)(2,1)}, u32[]{:S(2)}, u32[]{:S(2)}) async-start(bf16[16,1,32,2048]{3,2,1,0:T(8,128)(2,1)} %bitcast.169), calls=%async_computation | async-start | bytes 4194304 | tf_op jit(solution)/shard_map/all_to_all | solution.py:83
  76.9 192.5 %reduce-scatter.8.cloned.1.call-start = ((), (), s32[]{:S(2)}) async-start(), calls=%async_computation.9 | async-start | bytes 9437184 | tf_op jit(solution)/shard_map/reduce_scatter | solution.py:100
  118.1 4.4 copy-start.6
  127.6 0.9 copy-start.7
  134.6 163.3 %reduce-scatter.4.cloned.1.call-start = ((), (), s32[]{:S(2)}) async-start(), calls=%async_computation.7 | async-start | bytes 9437184 | tf_op jit(solution)/shard_map/reduce_scatter | solution.py:98
  141.0 236.6 %reduce-scatter.6.cloned.1.call-start = ((), (), s32[]{:S(2)}) async-start(), calls=%async_computation.8 | async-start | bytes 9437184 | tf_op jit(solution)/shard_map/reduce_scatter | solution.py:99
  153.1 52.8 %all-to-all-start.1 = ((bf16[16,1,32,2048]{3,2,1,0:T(8,128)(2,1)}), bf16[16,1,32,2048]{3,2,1,0:T(8,128)(2,1)}, u32[]{:S(2)}, u32[]{:S(2)}) async-start(bf16[16,1,32,2048]{3,2,1,0:T(8,128)(2,1)} %fusion.17), calls=%async_computation.1 | async-start | bytes 4194304 | tf_op jit(solution)/shard_map/all_to_all | solution.py:85
  164.7 4.0 copy-start.5
  205.9 52.4 %all-to-all-start.3 = ((bf16[16,1,32,2048]{3,2,1,0:T(8,128)(2,1)}), bf16[16,1,32,2048]{3,2,1,0:T(8,128)(2,1)}, u32[]{:S(2)}, u32[]{:S(2)}) async-start(bf16[16,1,32,2048]{3,2,1,0:T(8,128)(2,1)} %fusion.20), calls=%async_computation.3 | async-start | bytes 4194304 | tf_op jit(solution)/shard_map/all_to_all | solution.py:90
  217.2 229.2 %all-reduce.2.cloned.1.call-start = ((), (), s32[]{:S(2)}) async-start(), calls=%async_computation.10 | async-start | bytes 262144 | tf_op jit(solution)/shard_map/psum | solution.py:122
  217.4 5.4 %copy-start.3 = (bf16[32,2048]{1,0:T(8,128)(2,1)S(1)}, bf16[32,2048]{1,0:T(8,128)(2,1)}, u32[]{:S(2)}) copy-start(bf16[32,2048]{1,0:T(8,128)(2,1)} %param.11) | copy-start | bytes 393220
  258.3 5.2 %copy-start.4 = (s32[32,8]{0,1:T(8,128)S(1)}, s32[32,8]{0,1:T(8,128)}, u32[]{:S(2)}) copy-start(s32[32,8]{0,1:T(8,128)} %param.10) | copy-start | bytes 3076
  263.5 4.9 %copy-start.2 = (bf16[2048,16]{0,1:T(8,128)(2,1)S(1)}, bf16[2048,16]{0,1:T(8,128)(2,1)}, u32[]{:S(2)}) copy-start(bf16[2048,16]{0,1:T(8,128)(2,1)} %param.12) | copy-start | bytes 196612
Sparse Core Ops, SparseCore 0:
  134.7 83.5 reduce-scatter.7
  220.8 77.0 reduce-scatter.3
  300.2 77.2 reduce-scatter.5
Sparse Core Ops, SparseCore 1:
  268.6 177.8 all-reduce.1
where the time goes:
time: 456 us; the launch traced here: 455 us
  waiting for transfers between devices  309 us (68%)
  matrix products  57.6 us (13%)
  starting transfers between devices  42 us (9%)
  other arithmetic  17.2 us (4%)
  between operations  15.4 us (3%)
  local copies, waits for them, and re-layouts  13.5 us (3%)
    reduce_scatter x1, waiting for transfers between devices, local(): lax.psum_scatter(up_term, 'dp', scatter_dimension=1, tiled=True)  76.4 us
    psum x1, waiting for transfers between devices, local(): router_grad = lax.psum(router_term, ('dp', 'expert'))  65.6 us
    all_to_all x1, waiting for transfers between devices, local(): lax.all_to_all(send_grads, 'expert', split_axis=0, concat_axis=0, tiled=T...  39.1 us
    all_to_all x1, waiting for transfers between devices, local(): lax.all_to_all(send_rows, 'expert', split_axis=0, concat_axis=0, tiled=True)  35.6 us
    all_to_all x1, waiting for transfers between devices, local(): lax.all_to_all(expert_out, 'expert', split_axis=0, concat_axis=0, tiled=T...  34 us
    all_to_all x1, waiting for transfers between devices, local(): lax.all_to_all(input_grad, 'expert', split_axis=0, concat_axis=0, tiled=T...  33.4 us
    reduce_scatter x1, waiting for transfers between devices, local(): lax.psum_scatter(gate_term, 'dp', scatter_dimension=1, tiled=True)  25.2 us
    all_to_all x1, starting transfers between devices, local(): lax.all_to_all(expert_out, 'expert', split_axis=0, concat_axis=0, tiled=T...  11.6 us
  transfers between devices with their start and end apart: 8, of which 7 were waited for; matrix products, arithmetic and copies ran while one was open for 13% of the time, Pallas kernels for 0%

commit v1 on v0

--- a/solution.py
+++ b/solution.py
@@ -1,7 +1,27 @@
+import functools
 import jax
 import jax.numpy as jnp
 from jax import lax
 from jax.sharding import PartitionSpec as P
+
+
+def terms_shape(u_in, across):
+    w1, carry_in = (lax.axis_size(across), lax.axis_index(across))
+    side_arr = list(u_in.shape)
+    near = u_in.shape[0] // w1
+    side_arr[0] = near
+    top = side_arr[0]
+    side_arr[0] = top * w1
+    s_next = jnp.zeros(side_arr, u_in.dtype)
+    for to_i in range(w1):
+        e_next = lax.dynamic_slice_in_dim(u_in, (carry_in ^ to_i) * near, near, axis=0)
+        if to_i:
+            e_next = lax.ppermute(e_next, across, [(dev_i, dev_i ^ to_i) for dev_i in range(w1)])
+        s_next = lax.dynamic_update_slice_in_dim(s_next, e_next, (carry_in ^ to_i) * top, axis=0)
+    return s_next
+
+
+_work_panels = functools.partial(terms_shape, across="expert")
 
 
 def silu_parts(gate_act):
@@ -82,7 +102,7 @@
     )
     arrived = lax.all_to_all(send_rows, "expert", split_axis=0, concat_axis=0, tiled=True)
     expert_out, stored = expert_forward(arrived, gate_weight, up_weight, down_weight)
-    returned = lax.all_to_all(expert_out, "expert", split_axis=0, concat_axis=0, tiled=True)
+    returned = _work_panels(expert_out)
     arrived_grads = lax.all_to_all(send_grads, "expert", split_axis=0, concat_axis=0, tiled=True)
     input_grad, gate_part, up_part = expert_backward(
         arrived_grads, stored, gate_weight, up_weight, down_weight

time: 456 us -> 473 us (1.037)
  local copies, waits for them, and re-layouts: 13.5 us -> 33.4 us
  starting transfers between devices: 42 us -> 48.1 us
  waiting for transfers between devices: 309 us -> 303 us
    ppermute x0 -> x15, waiting for transfers between devices: none -> 76.4 us  [terms_shape(): lax.ppermute(e_next, across, [(dev_i, dev_i ^ to_i) for dev_i in range(w1)])]
    all_to_all x1 -> x0, waiting for transfers between devices: 34 us -> none  [local(): lax.all_to_all(expert_out, 'expert', split_axis=0, concat_axis=0, tiled=T...]
    all_to_all x1, waiting for transfers between devices: 33.4 us -> 0.01 us  [local(): lax.all_to_all(input_grad, 'expert', split_axis=0, concat_axis=0, tiled=T...]
    reduce_scatter x1, waiting for transfers between devices: 25.2 us -> 0.01 us  [local(): lax.psum_scatter(gate_term, 'dp', scatter_dimension=1, tiled=True)]
    ppermute x0 -> x15, starting transfers between devices: none -> 22.8 us  [terms_shape(): lax.ppermute(e_next, across, [(dev_i, dev_i ^ to_i) for dev_i in range(w1)])]
    psum x1, waiting for transfers between devices: 65.6 us -> 82.4 us  [local(): router_grad = lax.psum(router_term, ('dp', 'expert'))]
    dynamic_update_slice x0 -> x16, local copies, waits for them, and re-layouts: none -> 15.9 us  [terms_shape(): lax.dynamic_update_slice_in_dim(s_next, e_next, (carry_in ^ to_i) * top,...]
    all_to_all x1 -> x0, starting transfers between devices: 11.6 us -> none  [local(): lax.all_to_all(expert_out, 'expert', split_axis=0, concat_axis=0, tiled=T...]
  transfers between devices with their start and end apart: 8 -> 22, of which waited for: 7 -> 14; matrix products, arithmetic and copies ran while one was open for 13% -> 16% of each run, Pallas kernels for 0% -> 0%
where the time goes in v1:
time: 473 us; the launch traced here: 472 us
  waiting for transfers between devices  303 us (64%)
  matrix products  54 us (11%)
  starting transfers between devices  48.1 us (10%)
  local copies, waits for them, and re-layouts  33.4 us (7%)
  other arithmetic  17.5 us (4%)
  between operations  15.6 us (3%)
    psum x1, waiting for transfers between devices, local(): router_grad = lax.psum(router_term, ('dp', 'expert'))  82.4 us
    ppermute x15, waiting for transfers between devices, terms_shape(): lax.ppermute(e_next, across, [(dev_i, dev_i ^ to_i) for dev_i in range(w1)])  76.4 us
    reduce_scatter x1, waiting for transfers between devices, local(): lax.psum_scatter(up_term, 'dp', scatter_dimension=1, tiled=True)  69.5 us
    all_to_all x1, waiting for transfers between devices, local(): lax.all_to_all(send_grads, 'expert', split_axis=0, concat_axis=0, tiled=T...  39.1 us
    all_to_all x1, waiting for transfers between devices, local(): lax.all_to_all(send_rows, 'expert', split_axis=0, concat_axis=0, tiled=True)  35.6 us
    ppermute x15, starting transfers between devices, terms_shape(): lax.ppermute(e_next, across, [(dev_i, dev_i ^ to_i) for dev_i in range(w1)])  22.8 us
    dynamic_update_slice x16, local copies, waits for them, and re-layouts, terms_shape(): lax.dynamic_update_slice_in_dim(s_next, e_next, (carry_in ^ to_i) * top,...  15.9 us
    all_to_all x1, starting transfers between devices, local(): lax.all_to_all(send_rows, 'expert', split_axis=0, concat_axis=0, tiled=True)  11.3 us
  transfers between devices with their start and end apart: 22, of which 14 were waited for; matrix products, arithmetic and copies ran while one was open for 16% of the time, Pallas kernels for 0%

profile of v1, /device:TPU:0, one launch (start us, length us, event | category | flops | bytes accessed | tf_op | source)
XLA Modules:
  0.0 471.7 jit_solution(15565669161071847590)
XLA Ops:
  12.9 4.1 convolution_convert_fusion
  17.0 7.5 %all-to-all-start.1 = ((bf16[16,1,32,2048]{3,2,1,0:T(8,128)(2,1)}), bf16[16,1,32,2048]{3,2,1,0:T(8,128)(2,1)}, u32[]{:S(2)}, u32[]{:S(2)}) async-start(bf16[16,1,32,2048]{3,2,1,0:T(8,128)(2,1)} %bitcast.256), calls=%async_computation.1 | async-start | bytes 4194304 | tf_op jit(solution)/shard_map/all_to_all | solution.py:106
  26.6 39.1 %all-to-all-done.1 = bf16[16,1,32,2048]{3,2,1,0:T(8,128)(2,1)} async-done(((bf16[16,1,32,2048]{3,2,1,0:T(8,128)(2,1)}), bf16[16,1,32,2048]{3,2,1,0:T(8,128)(2,1)}, u32[]{:S(2)}, u32[]{:S(2)}) %all-to-all-start.1) | async-done | bytes 2097184 | tf_op jit(solution)/shard_map/all_to_all | solution.py:106
  65.7 11.3 %all-to-all-start = ((bf16[16,1,32,2048]{3,2,1,0:T(8,128)(2,1)}), bf16[16,1,32,2048]{3,2,1,0:T(8,128)(2,1)}, u32[]{:S(2)}, u32[]{:S(2)}) async-start(bf16[16,1,32,2048]{3,2,1,0:T(8,128)(2,1)} %bitcast.255), calls=%async_computation | async-start | bytes 4194304 | tf_op jit(solution)/shard_map/all_to_all | solution.py:103
  77.0 5.5 %fusion = f32[16,32,768]{2,1,0:T(8,128)} fusion(bf16[1,768,2048]{2,1,0:T(8,128)(2,1)} %param.15, bf16[16,1,32,2048]{3,2,1,0:T(8,128)(2,1)} %all-to-all-done.1), kind=kOutput, calls=%fused_computation.6 | convolution fusion | flops 1610612736 | bytes 6815744 | tf_op jit(solution)/shard_map/sjcd,jfd->sjcf/dot_general | solution.py:49
  82.5 35.6 %all-to-all-done = bf16[16,1,32,2048]{3,2,1,0:T(8,128)(2,1)} async-done(((bf16[16,1,32,2048]{3,2,1,0:T(8,128)(2,1)}), bf16[16,1,32,2048]{3,2,1,0:T(8,128)(2,1)}, u32[]{:S(2)}, u32[]{:S(2)}) %all-to-all-start) | async-done | bytes 2097184 | tf_op jit(solution)/shard_map/all_to_all | solution.py:103
  118.1 4.4 fusion.6
  122.6 5.1 %fusion.38 = (bf16[16,32,768]{2,1,0:T(8,128)(2,1)S(1)}, bf16[16,1,32,768]{3,2,0,1:T(8,128)(2,1)}, bf16[16,32,768]{2,1,0:T(8,128)(2,1)}) fusion(f32[16,32,768]{2,1,0:T(8,128)S(1)} %fusion.6, f32[16,32,768]{2,1,0:T(8,128)S(1)} %copy-done.20, bf16[1,2048,768]{2,1,0:T(8,128)(2,1)S(1)} %copy-done, bf16[16,1,32,2048]{3,2,1,0:T(8,128)(2,1)} %all-to-all-done), kind=kOutput, calls=%fused_computation.52 | convolution fusion | flops 1616510976 | bytes 10747904 | tf_op jit(solution)/shard_map/sjcd,jdf->sjcf/dot_general | solution.py:35
  128.5 6.1 %convolution_bitcast_fusion = f32[1,768,2048]{2,1,0:T(8,128)} fusion(bf16[16,32,768]{2,1,0:T(8,128)(2,1)S(1)} %get-tuple-element.13, bf16[16,1,32,2048]{3,2,1,0:T(8,128)(2,1)} %all-to-all-done.1), kind=kOutput, calls=%fused_computation.3 | convolution fusion | flops 1610612736 | bytes 9175040 | tf_op jit(solution)/shard_map/sjcf,sjcd->jfd/dot_general | solution.py:114
  134.7 6.2 %convolution_bitcast_fusion.2 = f32[1,2048,768]{2,1,0:T(8,128)} fusion(bf16[16,1,32,2048]{3,2,1,0:T(8,128)(2,1)} %all-to-all-done, bf16[16,1,32,768]{3,2,0,1:T(8,128)(2,1)} %get-tuple-element.14), kind=kOutput, calls=%fused_computation.5 | convolution fusion | flops 1610612736 | bytes 9175040 | tf_op jit(solution)/shard_map/sjcd,sjcf->jdf/dot_general | solution.py:112
  141.2 6.3 %convolution_bitcast_fusion.1 = f32[1,2048,768]{2,1,0:T(8,128)} fusion(bf16[16,32,768]{2,1,0:T(8,128)(2,1)} %get-tuple-element.15, bf16[16,1,32,2048]{3,2,1,0:T(8,128)(2,1)} %all-to-all-done), kind=kOutput, calls=%fused_computation.4 | convolution fusion | flops 1610612736 | bytes 9175040 | tf_op jit(solution)/shard_map/sjcd,sjcf->jdf/dot_general | solution.py:113
  147.8 4.2 fusion.12
  154.5 10.2 %collective-permute-start.14 = (bf16[1,1,32,2048]{3,2,0,1:T(8,128)(2,1)S(1)}, bf16[1,1,32,2048]{3,2,0,1:T(8,128)(2,1)}, u32[]{:S(2)}, u32[]{:S(2)}) collective-permute-start(bf16[1,1,32,2048]{3,2,0,1:T(8,128)(2,1)S(1)} %get-tuple-element.16), channel_id=1, source_target_pairs={{0,15},{1,14},{2,13},{3,12},{4,11},{5,10},{6,9},{7,8},{8,7},{9,6},... | collective-permute-start | bytes 393224 | tf_op jit(solution)/shard_map/ppermute | solution.py:19
  164.9 3.5 collective-permute-start.11
  173.5 6.0 %all-to-all-start.2 = ((bf16[16,1,32,2048]{3,2,1,0:T(8,128)(2,1)}), bf16[16,1,32,2048]{3,2,1,0:T(8,128)(2,1)}, u32[]{:S(2)}, u32[]{:S(2)}) async-start(bf16[16,1,32,2048]{3,2,1,0:T(8,128)(2,1)} %fusion.17), calls=%async_computation.2 | async-start | bytes 4194304 | tf_op jit(solution)/shard_map/all_to_all | solution.py:110
  186.5 13.4 %collective-permute-done.1 = bf16[1,1,32,2048]{3,2,0,1:T(8,128)(2,1)S(1)} collective-permute-done((bf16[1,1,32,2048]{3,2,0,1:T(8,128)(2,1)S(1)}, bf16[1,1,32,2048]{3,2,0,1:T(8,128)(2,1)S(1)}, u32[]{:S(2)}, u32[]{:S(2)}) %collective-permute-start.1) | collective-permute-done | bytes 131104 | tf_op jit(solution)/shard_map/ppermute | solution.py:19
  200.5 4.9 %collective-permute-done.2 = bf16[1,1,32,2048]{3,2,0,1:T(8,128)(2,1)S(1)} collective-permute-done((bf16[1,1,32,2048]{3,2,0,1:T(8,128)(2,1)S(1)}, bf16[1,1,32,2048]{3,2,0,1:T(8,128)(2,1)S(1)}, u32[]{:S(2)}, u32[]{:S(2)}) %collective-permute-start.2) | collective-permute-done | bytes 131104 | tf_op jit(solution)/shard_map/ppermute | solution.py:19
  206.0 11.2 %collective-permute-done.3 = bf16[1,1,32,2048]{3,2,0,1:T(8,128)(2,1)S(1)} collective-permute-done((bf16[1,1,32,2048]{3,2,0,1:T(8,128)(2,1)S(1)}, bf16[1,1,32,2048]{3,2,0,1:T(8,128)(2,1)S(1)}, u32[]{:S(2)}, u32[]{:S(2)}) %collective-permute-start.3) | collective-permute-done | bytes 131104 | tf_op jit(solution)/shard_map/ppermute | solution.py:19
  219.9 7.8 %collective-permute-done.4 = bf16[1,1,32,2048]{3,2,0,1:T(8,128)(2,1)S(1)} collective-permute-done((bf16[1,1,32,2048]{3,2,0,1:T(8,128)(2,1)S(1)}, bf16[1,1,32,2048]{3,2,0,1:T(8,128)(2,1)S(1)}, u32[]{:S(2)}, u32[]{:S(2)}) %collective-permute-start.4) | collective-permute-done | bytes 131104 | tf_op jit(solution)/shard_map/ppermute | solution.py:19
  229.5 4.7 collective-permute-done.5
  234.8 5.5 %collective-permute-done.6 = bf16[1,1,32,2048]{3,2,0,1:T(8,128)(2,1)S(1)} collective-permute-done((bf16[1,1,32,2048]{3,2,0,1:T(8,128)(2,1)S(1)}, bf16[1,1,32,2048]{3,2,0,1:T(8,128)(2,1)S(1)}, u32[]{:S(2)}, u32[]{:S(2)}) %collective-permute-start.6) | collective-permute-done | bytes 131104 | tf_op jit(solution)/shard_map/ppermute | solution.py:19
  240.3 3.8 collective-permute-start.7
  244.7 5.3 %collective-permute-done.7 = bf16[1,1,32,2048]{3,2,0,1:T(8,128)(2,1)S(1)} collective-permute-done((bf16[1,1,32,2048]{3,2,0,1:T(8,128)(2,1)S(1)}, bf16[1,1,32,2048]{3,2,0,1:T(8,128)(2,1)S(1)}, u32[]{:S(2)}, u32[]{:S(2)}) %collective-permute-start.7) | collective-permute-done | bytes 131104 | tf_op jit(solution)/shard_map/ppermute | solution.py:19
  250.7 7.2 %collective-permute-done.8 = bf16[1,1,32,2048]{3,2,0,1:T(8,128)(2,1)S(1)} collective-permute-done((bf16[1,1,32,2048]{3,2,0,1:T(8,128)(2,1)S(1)}, bf16[1,1,32,2048]{3,2,0,1:T(8,128)(2,1)S(1)}, u32[]{:S(2)}, u32[]{:S(2)}) %collective-permute-start.8) | collective-permute-done | bytes 131104 | tf_op jit(solution)/shard_map/ppermute | solution.py:19
  258.6 8.4 %collective-permute-done.9 = bf16[1,1,32,2048]{3,2,0,1:T(8,128)(2,1)S(1)} collective-permute-done((bf16[1,1,32,2048]{3,2,0,1:T(8,128)(2,1)S(1)}, bf16[1,1,32,2048]{3,2,0,1:T(8,128)(2,1)S(1)}, u32[]{:S(2)}, u32[]{:S(2)}) %collective-permute-start.9) | collective-permute-done | bytes 131104 | tf_op jit(solution)/shard_map/ppermute | solution.py:19
  267.7 8.0 %collective-permute-done.10 = bf16[1,1,32,2048]{3,2,0,1:T(8,128)(2,1)S(1)} collective-permute-done((bf16[1,1,32,2048]{3,2,0,1:T(8,128)(2,1)S(1)}, bf16[1,1,32,2048]{3,2,0,1:T(8,128)(2,1)S(1)}, u32[]{:S(2)}, u32[]{:S(2)}) %collective-permute-start.10) | collective-permute-done | bytes 131104 | tf_op jit(solution)/shard_map/ppermute | solution.py:19
  282.6 5.2 %gather_fusion = bf16[256,2048]{1,0:T(8,128)(2,1)} fusion(bf16[512,2048]{1,0:T(8,128)(2,1)} %bitcast.66, s32[1024]{0:T(1024)S(1)} %pad_clamp_fusion), kind=kCustom, calls=%fused_computation.clone | custom fusion | bytes 2098176 | tf_op jit(solution)/shard_map/jit(_take)/gather | solution.py:126
  291.1 5.2 %gather_fusion.1 = bf16[256,2048]{1,0:T(8,128)(2,1)} fusion(bf16[512,2048]{1,0:T(8,128)(2,1)} %bitcast.84, s32[1024]{0:T(1024)S(1)} %pad_clamp_fusion), kind=kCustom, calls=%fused_computation.1.clone | custom fusion | bytes 2098176 | tf_op jit(solution)/shard_map/jit(_take)/gather | solution.py:129
  296.3 4.0 convert_reduce_fusion
  304.5 3.5 convert_element_type.91
  308.0 69.5 %reduce-scatter.6.cloned.1.call-done = f32[1,1024,768]{2,1,0:T(8,128)} async-done(((f32[1,2048,768]{2,1,0:T(8,128)}), f32[1,1024,768]{2,1,0:T(8,128)}) %reduce-scatter.6.cloned.1.call-update) | async-done | bytes 3145744 | tf_op jit(solution)/shard_map/reduce_scatter | solution.py:119
  380.7 82.4 %all-reduce.2.cloned.1.call-done = f32[2048,16]{0,1:T(8,128)} async-done(((f32[2048,16]{0,1:T(8,128)}), f32[2048,16]{0,1:T(8,128)}) %all-reduce.2.cloned.1.call-update) | async-done | bytes 131088 | tf_op jit(solution)/shard_map/psum | solution.py:142
  (120 shorter events, 51.1 us)
Async XLA Ops:
  8.0 114.5 %copy-start = (bf16[1,2048,768]{2,1,0:T(8,128)(2,1)S(1)}, bf16[1,2048,768]{2,1,0:T(8,128)(2,1)}, u32[]{:S(2)}) copy-start(bf16[1,2048,768]{2,1,0:T(8,128)(2,1)} %param.13) | copy-start | bytes 9437188
  17.0 48.7 %all-to-all-start.1 = ((bf16[16,1,32,2048]{3,2,1,0:T(8,128)(2,1)}), bf16[16,1,32,2048]{3,2,1,0:T(8,128)(2,1)}, u32[]{:S(2)}, u32[]{:S(2)}) async-start(bf16[16,1,32,2048]{3,2,1,0:T(8,128)(2,1)} %bitcast.256), calls=%async_computation.1 | async-start | bytes 4194304 | tf_op jit(solution)/shard_map/all_to_all | solution.py:106
  65.7 52.4 %all-to-all-start = ((bf16[16,1,32,2048]{3,2,1,0:T(8,128)(2,1)}), bf16[16,1,32,2048]{3,2,1,0:T(8,128)(2,1)}, u32[]{:S(2)}, u32[]{:S(2)}) async-start(bf16[16,1,32,2048]{3,2,1,0:T(8,128)(2,1)} %bitcast.255), calls=%async_computation | async-start | bytes 4194304 | tf_op jit(solution)/shard_map/all_to_all | solution.py:103
  77.0 224.3 %reduce-scatter.8.cloned.1.call-start = ((), (), s32[]{:S(2)}) async-start(), calls=%async_computation.8 | async-start | bytes 9437184 | tf_op jit(solution)/shard_map/reduce_scatter | solution.py:120
  134.6 169.9 %reduce-scatter.4.cloned.1.call-start = ((), (), s32[]{:S(2)}) async-start(), calls=%async_computation.6 | async-start | bytes 9437184 | tf_op jit(solution)/shard_map/reduce_scatter | solution.py:118
  141.0 236.5 %reduce-scatter.6.cloned.1.call-start = ((), (), s32[]{:S(2)}) async-start(), calls=%async_computation.7 | async-start | bytes 9437184 | tf_op jit(solution)/shard_map/reduce_scatter | solution.py:119
  154.5 126.5 %collective-permute-start.14 = (bf16[1,1,32,2048]{3,2,0,1:T(8,128)(2,1)S(1)}, bf16[1,1,32,2048]{3,2,0,1:T(8,128)(2,1)}, u32[]{:S(2)}, u32[]{:S(2)}) collective-permute-start(bf16[1,1,32,2048]{3,2,0,1:T(8,128)(2,1)S(1)} %get-tuple-element.16), channel_id=1, source_target_pairs={{0,15},{1,14},{2,13},{3,12},{4,11},{5,10},{6,9},{7,8},{8,7},{9,6},... | collective-permute-start | bytes 393224 | tf_op jit(solution)/shard_map/ppermute | solution.py:19
  164.7 114.8 %collective-permute-start.13 = (bf16[1,1,32,2048]{3,2,0,1:T(8,128)(2,1)}, bf16[1,1,32,2048]{3,2,0,1:T(8,128)(2,1)}, u32[]{:S(2)}, u32[]{:S(2)}) collective-permute-start(bf16[1,1,32,2048]{3,2,0,1:T(8,128)(2,1)} %get-tuple-element.17), channel_id=1, source_target_pairs={{0,14},{1,15},{2,12},{3,13},{4,10},{5,11},{6,8},{7,9},{8,6},{9,7},... | collective-permute-start | bytes 393224 | tf_op jit(solution)/shard_map/ppermute | solution.py:19
  164.9 113.1 %collective-permute-start.12 = (bf16[1,1,32,2048]{3,2,0,1:T(8,128)(2,1)}, bf16[1,1,32,2048]{3,2,0,1:T(8,128)(2,1)}, u32[]{:S(2)}, u32[]{:S(2)}) collective-permute-start(bf16[1,1,32,2048]{3,2,0,1:T(8,128)(2,1)} %get-tuple-element.18), channel_id=1, source_target_pairs={{0,13},{1,12},{2,15},{3,14},{4,9},{5,8},{6,11},{7,10},{8,5},{9,4},... | collective-permute-start | bytes 393224 | tf_op jit(solution)/shard_map/ppermute | solution.py:19
  164.9 111.5 %collective-permute-start.11 = (bf16[1,1,32,2048]{3,2,0,1:T(8,128)(2,1)}, bf16[1,1,32,2048]{3,2,0,1:T(8,128)(2,1)}, u32[]{:S(2)}, u32[]{:S(2)}) collective-permute-start(bf16[1,1,32,2048]{3,2,0,1:T(8,128)(2,1)} %get-tuple-element.19), channel_id=1, source_target_pairs={{0,12},{1,13},{2,14},{3,15},{4,8},{5,9},{6,10},{7,11},{8,4},{9,5},... | collective-permute-start | bytes 393224 | tf_op jit(solution)/shard_map/ppermute | solution.py:19
  168.4 14.6 %collective-permute-start = (bf16[1,1,32,2048]{3,2,0,1:T(8,128)(2,1)}, bf16[1,1,32,2048]{3,2,0,1:T(8,128)(2,1)}, u32[]{:S(2)}, u32[]{:S(2)}) collective-permute-start(bf16[1,1,32,2048]{3,2,0,1:T(8,128)(2,1)} %get-tuple-element.30), channel_id=1, source_target_pairs={{0,1},{1,0},{2,3},{3,2},{4,5},{5,4},{6,7},{7,6},{8,9},{9,8},{10,11... | collective-permute-start | bytes 393224 | tf_op jit(solution)/shard_map/ppermute | solution.py:19
  173.5 117.6 %all-to-all-start.2 = ((bf16[16,1,32,2048]{3,2,1,0:T(8,128)(2,1)}), bf16[16,1,32,2048]{3,2,1,0:T(8,128)(2,1)}, u32[]{:S(2)}, u32[]{:S(2)}) async-start(bf16[16,1,32,2048]{3,2,1,0:T(8,128)(2,1)} %fusion.17), calls=%async_computation.2 | async-start | bytes 4194304 | tf_op jit(solution)/shard_map/all_to_all | solution.py:110
  179.5 283.5 %all-reduce.2.cloned.1.call-start = ((), (), s32[]{:S(2)}) async-start(), calls=%async_computation.9 | async-start | bytes 262144 | tf_op jit(solution)/shard_map/psum | solution.py:142
  179.8 20.0 %copy-start.13 = (bf16[1,1,32,2048]{3,2,0,1:T(8,128)(2,1)S(1)}, bf16[1,1,32,2048]{3,2,0,1:T(8,128)(2,1)}, u32[]{:S(2)}) copy-start(bf16[1,1,32,2048]{3,2,0,1:T(8,128)(2,1)} %get-tuple-element.28) | copy-start | bytes 393220
  179.8 25.6 %copy-start.12 = (bf16[1,1,32,2048]{3,2,0,1:T(8,128)(2,1)S(1)}, bf16[1,1,32,2048]{3,2,0,1:T(8,128)(2,1)}, u32[]{:S(2)}) copy-start(bf16[1,1,32,2048]{3,2,0,1:T(8,128)(2,1)} %get-tuple-element.27) | copy-start | bytes 393220
  179.8 37.5 %copy-start.11 = (bf16[1,1,32,2048]{3,2,0,1:T(8,128)(2,1)S(1)}, bf16[1,1,32,2048]{3,2,0,1:T(8,128)(2,1)}, u32[]{:S(2)}) copy-start(bf16[1,1,32,2048]{3,2,0,1:T(8,128)(2,1)} %get-tuple-element.26) | copy-start | bytes 393220
  179.8 47.9 %copy-start.10 = (bf16[1,1,32,2048]{3,2,0,1:T(8,128)(2,1)S(1)}, bf16[1,1,32,2048]{3,2,0,1:T(8,128)(2,1)}, u32[]{:S(2)}) copy-start(bf16[1,1,32,2048]{3,2,0,1:T(8,128)(2,1)} %get-tuple-element.25) | copy-start | bytes 393220
  179.8 54.3 %copy-start.9 = (bf16[1,1,32,2048]{3,2,0,1:T(8,128)(2,1)S(1)}, bf16[1,1,32,2048]{3,2,0,1:T(8,128)(2,1)}, u32[]{:S(2)}) copy-start(bf16[1,1,32,2048]{3,2,0,1:T(8,128)(2,1)} %get-tuple-element.24) | copy-start | bytes 393220
  179.8 60.4 %copy-start.8 = (bf16[1,1,32,2048]{3,2,0,1:T(8,128)(2,1)S(1)}, bf16[1,1,32,2048]{3,2,0,1:T(8,128)(2,1)}, u32[]{:S(2)}) copy-start(bf16[1,1,32,2048]{3,2,0,1:T(8,128)(2,1)} %get-tuple-element.23) | copy-start | bytes 393220
  179.9 70.2 %copy-start.7 = (bf16[1,1,32,2048]{3,2,0,1:T(8,128)(2,1)S(1)}, bf16[1,1,32,2048]{3,2,0,1:T(8,128)(2,1)}, u32[]{:S(2)}) copy-start(bf16[1,1,32,2048]{3,2,0,1:T(8,128)(2,1)} %get-tuple-element.22) | copy-start | bytes 393220
  179.9 78.1 %copy-start.6 = (bf16[1,1,32,2048]{3,2,0,1:T(8,128)(2,1)S(1)}, bf16[1,1,32,2048]{3,2,0,1:T(8,128)(2,1)}, u32[]{:S(2)}) copy-start(bf16[1,1,32,2048]{3,2,0,1:T(8,128)(2,1)} %get-tuple-element.21) | copy-start | bytes 393220
  179.9 87.2 %copy-start.5 = (bf16[1,1,32,2048]{3,2,0,1:T(8,128)(2,1)S(1)}, bf16[1,1,32,2048]{3,2,0,1:T(8,128)(2,1)}, u32[]{:S(2)}) copy-start(bf16[1,1,32,2048]{3,2,0,1:T(8,128)(2,1)} %get-tuple-element.20) | copy-start | bytes 393220
  183.0 16.8 %collective-permute-start.1 = (bf16[1,1,32,2048]{3,2,0,1:T(8,128)(2,1)S(1)}, bf16[1,1,32,2048]{3,2,0,1:T(8,128)(2,1)S(1)}, u32[]{:S(2)}, u32[]{:S(2)}) collective-permute-start(bf16[1,1,32,2048]{3,2,0,1:T(8,128)(2,1)S(1)} %copy-done.14), channel_id=1, source_target_pairs={{0,2},{1,3},{2,0},{3,1},{4,6},{5,7},{6,4},{7,5},{8,10},{9,11},{10,... | collective-permute-start | bytes 393224 | tf_op jit(solution)/shard_map/ppermute | solution.py:19
  199.8 5.6 %collective-permute-start.2 = (bf16[1,1,32,2048]{3,2,0,1:T(8,128)(2,1)S(1)}, bf16[1,1,32,2048]{3,2,0,1:T(8,128)(2,1)S(1)}, u32[]{:S(2)}, u32[]{:S(2)}) collective-permute-start(bf16[1,1,32,2048]{3,2,0,1:T(8,128)(2,1)S(1)} %copy-done.13), channel_id=1, source_target_pairs={{0,3},{1,2},{2,1},{3,0},{4,7},{5,6},{6,5},{7,4},{8,11},{9,10},{10,... | collective-permute-start | bytes 393224 | tf_op jit(solution)/shard_map/ppermute | solution.py:19
  205.4 11.9 %collective-permute-start.3 = (bf16[1,1,32,2048]{3,2,0,1:T(8,128)(2,1)S(1)}, bf16[1,1,32,2048]{3,2,0,1:T(8,128)(2,1)S(1)}, u32[]{:S(2)}, u32[]{:S(2)}) collective-permute-start(bf16[1,1,32,2048]{3,2,0,1:T(8,128)(2,1)S(1)} %copy-done.12), channel_id=1, source_target_pairs={{0,4},{1,5},{2,6},{3,7},{4,0},{5,1},{6,2},{7,3},{8,12},{9,13},{10,... | collective-permute-start | bytes 393224 | tf_op jit(solution)/shard_map/ppermute | solution.py:19
  217.3 10.4 %collective-permute-start.4 = (bf16[1,1,32,2048]{3,2,0,1:T(8,128)(2,1)S(1)}, bf16[1,1,32,2048]{3,2,0,1:T(8,128)(2,1)S(1)}, u32[]{:S(2)}, u32[]{:S(2)}) collective-permute-start(bf16[1,1,32,2048]{3,2,0,1:T(8,128)(2,1)S(1)} %copy-done.11), channel_id=1, source_target_pairs={{0,5},{1,4},{2,7},{3,6},{4,1},{5,0},{6,3},{7,2},{8,13},{9,12},{10,... | collective-permute-start | bytes 393224 | tf_op jit(solution)/shard_map/ppermute | solution.py:19
  227.7 6.4 %collective-permute-start.5 = (bf16[1,1,32,2048]{3,2,0,1:T(8,128)(2,1)S(1)}, bf16[1,1,32,2048]{3,2,0,1:T(8,128)(2,1)S(1)}, u32[]{:S(2)}, u32[]{:S(2)}) collective-permute-start(bf16[1,1,32,2048]{3,2,0,1:T(8,128)(2,1)S(1)} %copy-done.10), channel_id=1, source_target_pairs={{0,6},{1,7},{2,4},{3,5},{4,2},{5,3},{6,0},{7,1},{8,14},{9,15},{10,... | collective-permute-start | bytes 393224 | tf_op jit(solution)/shard_map/ppermute | solution.py:19
  234.1 6.2 %collective-permute-start.6 = (bf16[1,1,32,2048]{3,2,0,1:T(8,128)(2,1)S(1)}, bf16[1,1,32,2048]{3,2,0,1:T(8,128)(2,1)S(1)}, u32[]{:S(2)}, u32[]{:S(2)}) collective-permute-start(bf16[1,1,32,2048]{3,2,0,1:T(8,128)(2,1)S(1)} %copy-done.9), channel_id=1, source_target_pairs={{0,7},{1,6},{2,5},{3,4},{4,3},{5,2},{6,1},{7,0},{8,15},{9,14},{10,... | collective-permute-start | bytes 393224 | tf_op jit(solution)/shard_map/ppermute | solution.py:19
  240.3 9.8 %collective-permute-start.7 = (bf16[1,1,32,2048]{3,2,0,1:T(8,128)(2,1)S(1)}, bf16[1,1,32,2048]{3,2,0,1:T(8,128)(2,1)S(1)}, u32[]{:S(2)}, u32[]{:S(2)}) collective-permute-start(bf16[1,1,32,2048]{3,2,0,1:T(8,128)(2,1)S(1)} %copy-done.8), channel_id=1, source_target_pairs={{0,8},{1,9},{2,10},{3,11},{4,12},{5,13},{6,14},{7,15},{8,0},{9,1},... | collective-permute-start | bytes 393224 | tf_op jit(solution)/shard_map/ppermute | solution.py:19
  250.0 7.9 %collective-permute-start.8 = (bf16[1,1,32,2048]{3,2,0,1:T(8,128)(2,1)S(1)}, bf16[1,1,32,2048]{3,2,0,1:T(8,128)(2,1)S(1)}, u32[]{:S(2)}, u32[]{:S(2)}) collective-permute-start(bf16[1,1,32,2048]{3,2,0,1:T(8,128)(2,1)S(1)} %copy-done.7), channel_id=1, source_target_pairs={{0,9},{1,8},{2,11},{3,10},{4,13},{5,12},{6,15},{7,14},{8,1},{9,0},... | collective-permute-start | bytes 393224 | tf_op jit(solution)/shard_map/ppermute | solution.py:19
  257.9 9.1 %collective-permute-start.9 = (bf16[1,1,32,2048]{3,2,0,1:T(8,128)(2,1)S(1)}, bf16[1,1,32,2048]{3,2,0,1:T(8,128)(2,1)S(1)}, u32[]{:S(2)}, u32[]{:S(2)}) collective-permute-start(bf16[1,1,32,2048]{3,2,0,1:T(8,128)(2,1)S(1)} %copy-done.6), channel_id=1, source_target_pairs={{0,10},{1,11},{2,8},{3,9},{4,14},{5,15},{6,12},{7,13},{8,2},{9,3},... | collective-permute-start | bytes 393224 | tf_op jit(solution)/shard_map/ppermute | solution.py:19
  267.0 8.7 %collective-permute-start.10 = (bf16[1,1,32,2048]{3,2,0,1:T(8,128)(2,1)S(1)}, bf16[1,1,32,2048]{3,2,0,1:T(8,128)(2,1)S(1)}, u32[]{:S(2)}, u32[]{:S(2)}) collective-permute-start(bf16[1,1,32,2048]{3,2,0,1:T(8,128)(2,1)S(1)} %copy-done.5), channel_id=1, source_target_pairs={{0,11},{1,10},{2,9},{3,8},{4,15},{5,14},{6,13},{7,12},{8,3},{9,2},... | collective-permute-start | bytes 393224 | tf_op jit(solution)/shard_map/ppermute | solution.py:19
  (11 other events, 61.4 us)
Sparse Core Ops, SparseCore 0:
  134.8 83.5 reduce-scatter.7
  220.8 77.0 reduce-scatter.3
  300.2 77.2 reduce-scatter.5
Sparse Core Ops, SparseCore 1:
  291.2 171.8 all-reduce.1
